TPU v7x, 128 devices: a whole 4x4x4 slice. The times are simulated.
128 devices in a mesh: int: 16 (over y, x_lo, core), occ: 4 (over z), red: 2 (over x_hi).
Axes of the slice: x: 4 (x_hi: 2, x_lo: 2; x = x_hi * 2 + x_lo), y: 4, z: 4, core: 2. Of those that a mesh axis runs over, the one named last changes fastest.
Arguments:
- amplitudes: bfloat16 [4096, 12800], P('occ', ('red', 'int')), may hold values from -6 to 6
- integrals: bfloat16 [12800, 25600], P('red', 'int'), may hold values from -0.0546875 to 0.0546875
Outputs:
- ladder: bfloat16 [4096, 25600], P('occ', ('int', 'red'))
All inputs are finite; a program needn't handle non-finite values.
Results may differ from a plain program's by a relative error of at most 0.015.
Values may be sent and summed in bfloat16 or wider, within the bound.
A program may use at most 192 MiB of HBM per device.

v0:
```python
import jax
import jax.numpy as jnp
from jax import lax
from jax.sharding import PartitionSpec as P

OW = 64


def mirror_rows(values, occ_count, swapped):
    rows, width = values.shape
    cube = values.reshape(OW // occ_count, OW, width)
    cube = jnp.swapaxes(swapped(cube), 0, 1)
    return cube.reshape(rows, width)


def final_pairs(summed, occ_count):

    def swapped(cube):
        return lax.all_to_all(
            cube.astype(jnp.bfloat16), "occ", split_axis=1, concat_axis=0, tiled=True
        ).astype(cube.dtype)

    return (summed - mirror_rows(summed, occ_count, swapped)).astype(jnp.bfloat16)


def on_device(amplitudes, integrals):
    occ_count = lax.axis_size("occ")
    partial_sum = jnp.dot(
        lax.all_gather(amplitudes, "int", axis=1, tiled=True),
        integrals,
        preferred_element_type=jnp.float32,
    )
    summed = lax.psum_scatter(
        partial_sum.astype(jnp.bfloat16), "red", scatter_dimension=1, tiled=True
    ).astype(jnp.float32)
    return final_pairs(summed, occ_count)


def solution(mesh):
    placed = (P("occ", ("red", "int")), P("red", "int"))
    return jax.shard_map(
        on_device, mesh=mesh, in_specs=placed, out_specs=P("occ", ("int", "red")), check_vma=False
    )
```

profile of v0, /device:TPU:0, one launch (start us, length us, event | category | flops | bytes accessed | tf_op | source)
XLA Modules:
  0.0 214.4 jit_solution(3739798794129435035)
XLA Ops:
  6.5 0.0 all-gather.2.cloned.1.call-start
  6.5 0.7 all-gather.2.cloned.1.call-update
  7.3 0.0 reduce-scatter.2.cloned.1.call-start
  7.3 78.6 %all-gather.2.cloned.1.call-done = bf16[1024,6400]{0,1:T(8,128)(2,1)} async-done(((bf16[1024,400]{0,1:T(8,128)(2,1)}), bf16[1024,6400]{0,1:T(8,128)(2,1)}) %all-gather.2.cloned.1.call-update) | async-done | bytes 13107216 | tf_op jit(solution)/shard_map/all_gather | solution.py:29
  85.9 29.0 %convolution_convert_fusion = bf16[1024,1600]{0,1:T(8,128)(2,1)} fusion(bf16[6400,1600]{0,1:T(8,128)(2,1)} %param.3, bf16[1024,6400]{0,1:T(8,128)(2,1)} %all-gather.2.cloned.1.call-done), kind=kOutput, calls=%fused_computation | convolution fusion | flops 20973158400 | bytes 36864000 | tf_op jit(solution)/shard_map/dot_general | solution.py:28
  114.9 0.0 reduce-scatter.2.cloned.1.call-update
  114.9 49.9 %reduce-scatter.2.cloned.1.call-done = bf16[1024,800]{0,1:T(8,128)(2,1)} async-done(((bf16[1024,1600]{0,1:T(8,128)(2,1)}), bf16[1024,800]{0,1:T(8,128)(2,1)}) %reduce-scatter.2.cloned.1.call-update) | async-done | bytes 1638416 | tf_op jit(solution)/shard_map/reduce_scatter | solution.py:33
  164.8 3.0 %copy.8 = bf16[1024,800]{1,0:T(8,128)(2,1)S(1)} copy(bf16[1024,800]{0,1:T(8,128)(2,1)} %reduce-scatter.2.cloned.1.call-done) | data formatting | bytes 3276800 | tf_op jit(solution)/shard_map/reduce_scatter | solution.py:33
  167.8 1.0 copy.9
  168.9 27.7 %all_to_all.4 = bf16[16,64,800]{2,0,1:T(8,128)(2,1)S(1)} all-to-all(bf16[16,64,800]{2,0,1:T(8,128)(2,1)S(1)} %copy.9), channel_id=1, replica_groups=mesh['int'=16,'occ'=4,'red'=2] {'occ'}, dimensions={1} | all-to-all | bytes 3276800 | tf_op jit(solution)/shard_map/all_to_all | solution.py:19
  196.6 0.4 copy.10
  197.0 0.4 convert_bitcast_fusion
  197.4 0.3 copy.11
  197.8 2.9 %copy.12 = f32[16,64,800]{2,1,0:T(8,128)} copy(f32[16,64,800]{2,0,1:T(8,128)S(1)} %bitcast.11) | data formatting | bytes 6553600 | tf_op jit(solution)/shard_map/reshape | solution.py:13
  200.7 3.6 %copy.13 = f32[1024,800]{0,1:T(8,128)S(1)} copy(f32[1024,800]{1,0:T(8,128)} %bitcast.12) | data formatting | bytes 6553600 | tf_op jit(solution)/shard_map/reshape | solution.py:13
  204.3 3.2 %subtract_convert_fusion = bf16[1024,800]{0,1:T(8,128)(2,1)} fusion(f32[1024,800]{0,1:T(8,128)S(1)} %copy.13, bf16[1024,800]{0,1:T(8,128)(2,1)} %reduce-scatter.2.cloned.1.call-done), kind=kLoop, calls=%fused_computation.2 | loop fusion | flops 2457600 | bytes 6553600 | tf_op jit(solution)/shard_map/convert_element_type | solution.py:23
Async XLA Ops:
  6.5 79.3 %all-gather.2.cloned.1.call-start = ((), (), s32[]{:S(2)}) async-start(), calls=%async_computation.2 | async-start | bytes 13926400 | tf_op jit(solution)/shard_map/all_gather | solution.py:29
  7.3 157.5 %reduce-scatter.2.cloned.1.call-start = ((), (), s32[]{:S(2)}) async-start(), calls=%async_computation.3 | async-start | bytes 4915200 | tf_op jit(solution)/shard_map/reduce_scatter | solution.py:33
Sparse Core Ops, SparseCore 0:
  9.1 76.7 all-gather.1
  115.0 49.7 reduce-scatter.1
where the time goes:
time: 215 us; the launch traced here: 214 us
  waiting for transfers between devices  129 us (60%)
  matrix products  29 us (13%)
  blocking collectives  27.7 us (13%)
  between operations  13.4 us (6%)
  local copies, waits for them, and re-layouts  11.3 us (5%)
  other arithmetic  3.58 us (2%)
    all_gather x1, waiting for transfers between devices, on_device(): lax.all_gather(amplitudes, 'int', axis=1, tiled=True)  78.6 us
    reduce_scatter x1, waiting for transfers between devices, on_device(): lax.psum_scatter(partial_sum.astype(jnp.bfloat16), 'red', scatter_dimensi...  49.9 us
    dot_general x1, matrix products, on_device(): jnp.dot(lax.all_gather(amplitudes, 'int', axis=1, tiled=True), integrals,...  29 us
    all_to_all x1, blocking collectives, swapped(): lax.all_to_all(cube.astype(jnp.bfloat16), 'occ', split_axis=1, concat_axi...  27.7 us
    reshape x3, local copies, waits for them, and re-layouts, mirror_rows(): return cube.reshape(rows, width)  6.88 us
  transfers between devices with their start and end apart: 2, of which 2 were waited for; matrix products, arithmetic and copies ran while one was open for 0% of the time, Pallas kernels for 0%

commit v1 on v0

v1 whole, which is shorter than its diff:
```python
import functools

import jax
import jax.numpy as jnp
from jax import lax
from jax.experimental import pallas as pl
from jax.experimental.pallas import tpu as pltpu
from jax.sharding import PartitionSpec as P

MESH = pl.DeviceIdType.MESH
F32, BF16, I32 = jnp.float32, jnp.bfloat16, jnp.int32

LANES = 128
CHUNK = 400
GROUP = 1600
WINDOW = 1664
HALF = 800
OCC = 1024
DZ = (1, 3, 2, 0)
MIRROR = (1, 0, 2)
DY = (0, 1, 3, 2)
STAGES = ((3, 0), (1, 2))


def dot(a, b, dims=((1,), (0,))):
    return lax.dot_general(a, b, (dims, ((), ())), preferred_element_type=F32)


def kernel(
    t_hbm, v_hbm, out, tv, vv, sel, own, zs, zr, at, acc, rs, rr, lad,
    load_sem, zs_sem, zr_sem, as_sem, ar_sem, rs_sem, rr_sem, ls_sem, lr_sem,
):
    index, z, xh = lax.axis_index("int"), lax.axis_index("occ"), lax.axis_index("red")
    y, xl, c = index // 4, (index // 2) % 2, index % 2

    def device(dy=0, flip_x=0, flip_c=0, dz=0, flip_red=0):
        there = ((y + dy) % 4) * 4 + (xl ^ flip_x) * 2 + (c ^ flip_c)
        return {"int": there, "occ": (z + dz) % 4, "red": xh ^ flip_red}

    load_t = pltpu.make_async_copy(t_hbm, tv, load_sem.at[0])
    load_v = pltpu.make_async_copy(v_hbm, vv, load_sem.at[1])
    load_t.start()
    load_v.start()

    barrier = pltpu.get_barrier_semaphore()
    partners = [device(dy=1), device(dy=2), device(dy=3), device(dz=1), device(dz=2), device(dz=3)]
    partners += [device(flip_x=1), device(flip_c=1), device(flip_red=1)]
    for partner in partners:
        pl.semaphore_signal(barrier, inc=1, device_id=partner, device_id_type=MESH)

    pair = lax.broadcasted_iota(I32, (1, LANES), 1)
    row = lax.broadcasted_iota(I32, (OCC, LANES), 0)

    def pairs_of(owner_is_lower):
        a = jnp.where(owner_is_lower, pair >> 4, pair >> 3)
        b = jnp.where(owner_is_lower, pair & 15, 8 + (pair & 7))
        return a, b

    for b in range(3):
        other = (z + DZ[b]) % 4
        p, q = pairs_of(z < other)
        sel[b] = jnp.where(row == p * 64 + other * 16 + q, 1.0, 0.0).astype(BF16)
        p, q = pairs_of(other < z)
        sel[4 + b] = jnp.where(row == q * 64 + other * 16 + p, -1.0, 0.0).astype(BF16)
    p = pair & 15
    q = (p + 1 + (pair >> 4)) & 15
    plus = jnp.where(pair < 120, p * 64 + z * 16 + q, -1)
    minus = jnp.where(pair < 120, q * 64 + z * 16 + p, -1)
    sel[3] = (jnp.where(row == plus, 1.0, 0.0) - jnp.where(row == minus, 1.0, 0.0)).astype(BF16)

    for b in range(4):
        for g in range(4):
            start = GROUP if g % 2 == 0 else 0
            at[b, g, start : start + WINDOW - GROUP, :] = jnp.zeros((WINDOW - GROUP, LANES), BF16)

    pl.semaphore_wait(barrier, len(partners))
    load_t.wait()

    sends = []

    def send(src, dst, send_sem, recv_sem, to):
        copy = pltpu.make_async_remote_copy(
            src_ref=src, dst_ref=dst, send_sem=send_sem, recv_sem=recv_sem, device_id=to, device_id_type=MESH
        )
        copy.start()
        sends.append(copy)

    def landed(ref, recv_sem):
        pltpu.make_async_copy(ref, ref, recv_sem).wait()

    def chunk(b, dy, rel):
        g = (y + dy) % 4
        start = 64 * (g % 2) + CHUNK * ((xl ^ (rel >> 1)) * 2 + (c ^ (rel & 1)))
        return at.at[b, g, pl.ds(pl.multiple_of(start, 16), CHUNK), :]

    def pass_on(b, n, dy, rel, to_dy, to_rel, to):
        ref = chunk(b, dy, rel)
        send(ref, ref, as_sem.at[b, n], ar_sem.at[b, to_dy, to_rel], to)

    def along_y(b, n, rel):
        for k, dy in enumerate((1, 3, 2)):
            pass_on(b, n + k, 0, rel, (-dy) % 4, rel, device(dy=dy))

    def send_own(b):
        pass_on(b, 0, 0, 0, 0, 2, device(flip_x=1))
        along_y(b, 1, 0)
        pass_on(b, 4, 0, 0, 0, 1, device(flip_c=1))

    def send_neighbours(b):
        landed(chunk(b, 0, 2), ar_sem.at[b, 0, 2])
        along_y(b, 5, 2)
        pass_on(b, 8, 0, 2, 0, 3, device(flip_c=1))

    def share(b, dy):
        for k, rel in enumerate((0, 2)):
            landed(chunk(b, dy, rel), ar_sem.at[b, dy, rel])
            pass_on(b, 9 + 2 * (dy - 1) + k, dy, rel, dy, rel + 1, device(flip_c=1))

    for b in range(3):
        zs[b] = dot(tv[...], sel[4 + b]).astype(BF16)
        send(zs.at[b], zr.at[MIRROR[b]], zs_sem.at[b], zr_sem.at[MIRROR[b]], device(dz=DZ[b]))

    order = [b for stage in STAGES for b in stage]
    here = pl.ds(pl.multiple_of(64 * (y % 2) + CHUNK * (xl * 2 + c), 16), CHUNK)
    for b in range(4):
        own[b] = dot(tv[...], sel[b])
    for b in order:
        if b < 3:
            landed(zr.at[b], zr_sem.at[b])
            at[b, y, here, :] = (own[b] + zr[b].astype(F32)).astype(BF16)
        else:
            at[b, y, here, :] = own[b].astype(BF16)
        send_own(b)
    for b in order:
        send_neighbours(b)

    load_v.wait()

    mine = pl.ds(pl.multiple_of(xh * HALF, 16), HALF)
    theirs = pl.ds(pl.multiple_of((1 - xh) * HALF, 16), HALF)

    def finish(stage):
        for k, b in enumerate(STAGES[stage]):
            landed(rr.at[b], rr_sem.at[b])
            lanes = slice(k * LANES, (k + 1) * LANES)
            lad[b] = (acc[stage, mine, lanes] + rr[b].astype(F32)).astype(BF16)
            if b < 3:
                m = MIRROR[b]
                send(lad.at[b], lad.at[4 + m], ls_sem.at[b], lr_sem.at[m], device(dz=DZ[b]))

    events = [(s, dy) for s in range(len(STAGES)) for dy in DY]
    for n, (s, dy) in enumerate(events):
        if n + 1 < len(events):
            s_next, dy_next = events[n + 1]
            if dy_next:
                for b in STAGES[s_next]:
                    share(b, dy_next)
        for b in STAGES[s]:
            for rel in (1, 3):
                landed(chunk(b, dy, rel), ar_sem.at[b, dy, rel])
        g = (y + dy) % 4
        window = pl.ds(pl.multiple_of(g * GROUP - 64 * (g % 2), 128), WINDOW)
        amplitudes = jnp.concatenate([at[b, g] for b in STAGES[s]], axis=1)
        for half in (theirs, mine):
            product = dot(vv[half, window], amplitudes)
            total = product if dy == DY[0] else acc[s, half, :] + product
            if dy == DY[-1] and half is theirs:
                for k, b in enumerate(STAGES[s]):
                    rs[b] = total[:, k * LANES : (k + 1) * LANES].astype(BF16)
                    send(rs.at[b], rr.at[b], rs_sem.at[b], rr_sem.at[b], device(flip_red=1))
            else:
                acc[s, half, :] = total
        if dy == DY[1] and s > 0:
            finish(s - 1)
    finish(len(STAGES) - 1)

    for b in range(3):
        landed(lad.at[4 + b], lr_sem.at[b])
    parts = jnp.concatenate([lad[b] for b in range(7)], axis=1)
    for n in range(0, OCC, 256):
        places = jnp.concatenate([sel[b, n : n + 256, :] for b in range(7)], axis=1)
        out[:, n : n + 256] = dot(parts, places, ((1,), (1,))).astype(BF16)

    for copy in sends:
        copy.wait_send()


def on_device(amplitudes, integrals):
    dma = pltpu.SemaphoreType.DMA
    stages = len(STAGES)
    width = max(len(stage) for stage in STAGES) * LANES
    ladder = pl.pallas_call(
        kernel,
        out_shape=jax.ShapeDtypeStruct((HALF, OCC), BF16),
        in_specs=[pl.BlockSpec(memory_space=pl.ANY)] * 2,
        out_specs=pl.BlockSpec(memory_space=pltpu.VMEM),
        scratch_shapes=[
            pltpu.VMEM((CHUNK, OCC), BF16),
            pltpu.VMEM((2 * HALF, 4 * GROUP), BF16),
            pltpu.VMEM((7, OCC, LANES), BF16),
            pltpu.VMEM((4, CHUNK, LANES), F32),
            pltpu.VMEM((3, CHUNK, LANES), BF16),
            pltpu.VMEM((3, CHUNK, LANES), BF16),
            pltpu.VMEM((4, 4, WINDOW, LANES), BF16),
            pltpu.VMEM((stages, 2 * HALF, width), F32),
            pltpu.VMEM((4, HALF, LANES), BF16),
            pltpu.VMEM((4, HALF, LANES), BF16),
            pltpu.VMEM((7, HALF, LANES), BF16),
            dma((2,)), dma((3,)), dma((3,)), dma((4, 15)), dma((4, 4, 4)), dma((4,)), dma((4,)), dma((3,)), dma((3,)),
        ],
        compiler_params=pltpu.CompilerParams(
            collective_id=0, has_side_effects=True, vmem_limit_bytes=52 * 2**20
        ),
        name="ladder",
    )(amplitudes.T, integrals.T)
    return ladder.T


def solution(mesh):
    placed = (P("occ", ("red", "int")), P("red", "int"))
    return jax.shard_map(
        on_device, mesh=mesh, in_specs=placed, out_specs=P("occ", ("int", "red")), check_vma=False
    )
```

time: 215 us -> 85.2 us (0.40)
  waiting for transfers between devices: 129 us -> 0 us
  Pallas kernels: 0 us -> 80.8 us
  matrix products: 29 us -> 0 us
  blocking collectives: 27.7 us -> 0 us
  between operations: 13.4 us -> 0.01 us
  local copies, waits for them, and re-layouts: 11.3 us -> 3.86 us
  other arithmetic: 3.58 us -> 0 us
    pallas_call x0 -> x1, Pallas kernels: none -> 80.8 us  [on_device(): pl.pallas_call(kernel, out_shape=jax.ShapeDtypeStruct((HALF, OCC), BF16),...]
    all_gather x1 -> x0, waiting for transfers between devices: 78.6 us -> none  [on_device(): lax.all_gather(amplitudes, 'int', axis=1, tiled=True)]
    reduce_scatter x1 -> x0, waiting for transfers between devices: 49.9 us -> none  [on_device(): lax.psum_scatter(partial_sum.astype(jnp.bfloat16), 'red', scatter_dimensi...]
    dot_general x1 -> x0, matrix products: 29 us -> none  [on_device(): jnp.dot(lax.all_gather(amplitudes, 'int', axis=1, tiled=True), integrals,...]
    all_to_all x1 -> x0, blocking collectives: 27.7 us -> none  [swapped(): lax.all_to_all(cube.astype(jnp.bfloat16), 'occ', split_axis=1, concat_axi...]
    reshape x3 -> x0, local copies, waits for them, and re-layouts: 6.88 us -> none  [mirror_rows(): return cube.reshape(rows, width)]
    unnamed x0 -> x3, local copies, waits for them, and re-layouts: none -> 3.86 us
    convert_element_type x1 -> x0, other arithmetic: 3.19 us -> none  [final_pairs(): (summed - mirror_rows(summed, occ_count, swapped)).astype(jnp.bfloat16)]
  transfers between devices with their start and end apart: 2 -> 0, of which waited for: 2 -> 0; matrix products, arithmetic and copies ran while one was open for 0% -> 0% of each run, Pallas kernels for 0% -> 0%
where the time goes in v1:
time: 85.2 us; the launch traced here: 84.7 us
  Pallas kernels  80.8 us (95%)
  local copies, waits for them, and re-layouts  3.86 us (5%)
    pallas_call x1, Pallas kernels, on_device(): pl.pallas_call(kernel, out_shape=jax.ShapeDtypeStruct((HALF, OCC), BF16),...  80.8 us
    unnamed x3, local copies, waits for them, and re-layouts  3.86 us

profile of v1, /device:TPU:0, one launch (start us, length us, event | category | flops | bytes accessed | tf_op | source)
XLA Modules:
  0.0 84.7 jit_solution(10949522620863336894)
XLA Ops:
  0.0 0.0 copy-start
  0.0 1.1 %copy-done = bf16[1024,400]{0,1:T(8,128)(2,1)S(1)} copy-done((bf16[1024,400]{0,1:T(8,128)(2,1)S(1)}, bf16[1024,400]{0,1:T(8,128)(2,1)}, u32[]{:S(2)}) %copy-start) | copy-done | bytes 819224
  1.1 80.8 %ladder.1 = bf16[800,1024]{1,0:T(8,128)(2,1)} custom-call(bf16[400,1024]{1,0:T(8,128)(2,1)S(1)} %bitcast.3, bf16[1600,6400]{1,0:T(8,128)(2,1)} %bitcast.4), custom_call_target="tpu_custom_call" | custom-call | tf_op jit(solution)/shard_map/ladder/pallas_call | solution.py:192
  81.9 2.7 %copy.4 = bf16[1024,800]{0,1:T(8,128)(2,1)} copy(bf16[1024,800]{0,1:T(8,128)(2,1)} %bitcast.5) | data formatting | bytes 3276800
Async XLA Ops:
  0.0 1.1 %copy-start = (bf16[1024,400]{0,1:T(8,128)(2,1)S(1)}, bf16[1024,400]{0,1:T(8,128)(2,1)}, u32[]{:S(2)}) copy-start(bf16[1024,400]{0,1:T(8,128)(2,1)} %param.2) | copy-start | bytes 2457604

commit v2 on v0

v2 whole, which is shorter than its diff:
```python
import functools

import jax
import jax.numpy as jnp
from jax import lax
from jax.experimental import pallas as pl
from jax.experimental.pallas import tpu as pltpu
from jax.sharding import PartitionSpec as P

MESH = pl.DeviceIdType.MESH
F32, BF16, I32 = jnp.float32, jnp.bfloat16, jnp.int32

LANES = 128
CHUNK = 400
GROUP = 1600
SLAB = 1280
HALF = 800
PART = 400
OCC = 1024
DZ = (1, 3, 2, 0)
MIRROR = (1, 0, 2)
DIAG = 3


def dot(a, b, dims=((1,), (0,))):
    return lax.dot_general(a, b, (dims, ((), ())), preferred_element_type=F32)


def kernel(
    t_hbm, v_hbm, out, tv, vv, slabs, sel, own, zs, zr, at, acc, total, rs, rr, lad,
    load_sem, zs_sem, zr_sem, as_sem, ar_sem, ds_sem, dr_sem, rs_sem, rr_sem, ls_sem, lr_sem,
):
    index, z, xh = lax.axis_index("int"), lax.axis_index("occ"), lax.axis_index("red")
    y, xl, c = index // 4, (index // 2) % 2, index % 2

    def device(dy=0, flip_x=0, flip_c=0, dz=0, flip_red=0):
        there = ((y + dy) % 4) * 4 + (xl ^ flip_x) * 2 + (c ^ flip_c)
        return {"int": there, "occ": (z + dz) % 4, "red": xh ^ flip_red}

    load_t = pltpu.make_async_copy(t_hbm, tv, load_sem.at[0])
    load_v = [
        pltpu.make_async_copy(v_hbm.at[:, n * SLAB : (n + 1) * SLAB], slabs.at[n % 2], load_sem.at[1 + n % 2])
        for n in range(4 * GROUP // SLAB)
    ]
    load_t.start()
    load_v[0].start()
    load_v[1].start()

    barrier = pltpu.get_barrier_semaphore()
    partners = [device(dy=1), device(dy=3), device(dz=1), device(dz=2), device(dz=3)]
    partners += [device(flip_x=1), device(flip_c=1), device(flip_red=1)]
    for partner in partners:
        pl.semaphore_signal(barrier, inc=1, device_id=partner, device_id_type=MESH)

    pair = lax.broadcasted_iota(I32, (1, LANES), 1)
    row = lax.broadcasted_iota(I32, (OCC, LANES), 0)

    def pairs_of(owner_is_lower):
        a = jnp.where(owner_is_lower, pair >> 4, pair >> 3)
        b = jnp.where(owner_is_lower, pair & 15, 8 + (pair & 7))
        return a, b

    def select_kept(b):
        other = (z + DZ[b]) % 4
        p, q = pairs_of(z < other)
        sel[b] = jnp.where(row == p * 64 + other * 16 + q, 1.0, 0.0).astype(BF16)

    def select_given(b):
        other = (z + DZ[b]) % 4
        p, q = pairs_of(other < z)
        sel[4 + b] = jnp.where(row == q * 64 + other * 16 + p, -1.0, 0.0).astype(BF16)

    def select_diagonal():
        p = pair & 15
        q = (p + 1 + (pair >> 4)) & 15
        plus = jnp.where(pair < 120, p * 64 + z * 16 + q, -1)
        minus = jnp.where(pair < 120, q * 64 + z * 16 + p, -1)
        sel[DIAG] = (jnp.where(row == plus, 1.0, 0.0) - jnp.where(row == minus, 1.0, 0.0)).astype(BF16)

    def turn(n):
        load_v[n].wait()

        def lanes(k, carry):
            first = pl.multiple_of(k * 128, 128)
            vv[pl.ds(n * SLAB + first, 128), :] = slabs[n % 2, :, pl.ds(first, 128)].T
            return carry

        lax.fori_loop(0, SLAB // 128, lanes, 0, unroll=2)
        if n + 2 < len(load_v):
            load_v[n + 2].start()

    sends = []

    def send(src, dst, send_sem, recv_sem, to):
        copy = pltpu.make_async_remote_copy(
            src_ref=src, dst_ref=dst, send_sem=send_sem, recv_sem=recv_sem, device_id=to, device_id_type=MESH
        )
        copy.start()
        sends.append(copy)

    def landed(ref, recv_sem):
        pltpu.make_async_copy(ref, ref, recv_sem).wait()

    def chunk(b, dy, rel, part=None):
        g = (y + dy) % 4
        start = CHUNK * ((xl ^ (rel >> 1)) * 2 + (c ^ (rel & 1)))
        first, rows = (0, CHUNK) if part is None else (part * 208, 208 - 16 * part)
        return at.at[b, g, pl.ds(pl.multiple_of(start + first, 16), rows), :]

    def pass_on(b, n, dy, rel, to_dy, to_rel, to):
        ref = chunk(b, dy, rel)
        send(ref, ref, as_sem.at[b, n], ar_sem.at[b, to_dy, to_rel], to)

    here = pl.ds(pl.multiple_of(CHUNK * (xl * 2 + c), 16), CHUNK)

    def to_next(b, rel):
        pass_on(b, 1 + 4 * (rel // 2), 0, rel, 3, rel, device(dy=1))

    def to_previous(b, rel):
        pass_on(b, 2 + 4 * (rel // 2), 0, rel, 1, rel, device(dy=3))

    def to_neighbours(b):
        pass_on(b, 0, 0, 0, 0, 2, device(flip_x=1))
        pass_on(b, 3, 0, 0, 0, 1, device(flip_c=1))

    def from_x(b, dy=0):
        landed(chunk(b, dy, 2), ar_sem.at[b, dy, 2])
        pass_on(b, 4 if dy == 0 else 8 + 2 * (dy - 1), dy, 2, dy, 3, device(flip_c=1))

    def share(b, dy, rel):
        landed(chunk(b, dy, rel), ar_sem.at[b, dy, rel])
        pass_on(b, 7 + 2 * (dy - 1) + rel // 2, dy, rel, dy, rel + 1, device(flip_c=1))

    def forward_next(b):
        pass_on(b, 13, 3, 0, 2, 0, device(dy=1))

    def forward_previous(b):
        pass_on(b, 14, 1, 2, 2, 2, device(dy=3))

    def across(dy):
        pass_on(DIAG, (13, 5, 6)[dy - 1], dy, 0, dy, 2, device(flip_x=1))

    def forward_diagonal(dy, k, to):
        ref = chunk(DIAG, dy, 0, k)
        send(ref, ref, ds_sem.at[k], dr_sem.at[k], to)

    def share_diagonal():
        for k in range(2):
            landed(chunk(DIAG, 2, 0, k), dr_sem.at[k])
        across(2)
        pass_on(DIAG, 9, 2, 0, 2, 1, device(flip_c=1))

    mine = xh * HALF
    theirs = (1 - xh) * HALF

    def multiply(b, dy):
        for rel in (1, 3):
            landed(chunk(b, dy, rel), ar_sem.at[b, dy, rel])
        g = (y + dy) % 4
        rows = pl.ds(pl.multiple_of(g * GROUP, 16), GROUP)
        product = dot(at[b, g].T, vv[rows, :])
        if dy == 0:
            acc[b] = product
        elif dy != 2:
            acc[b] += product
        else:
            total[b] = (acc[b] + product).T
            for h in range(2):
                rs[b, h] = total[b, pl.ds(pl.multiple_of(theirs + h * PART, 16), PART), :].astype(BF16)
                if b != DIAG:
                    reduce(b, h)

    def reduce(b, h):
        send(rs.at[b, h], rr.at[b, h], rs_sem.at[b, h], rr_sem.at[b, h], device(flip_red=1))

    def finish(b, h):
        landed(rr.at[b, h], rr_sem.at[b, h])
        rows = pl.ds(pl.multiple_of(mine + h * PART, 16), PART)
        lad[b, h] = (total[b, rows, :] + rr[b, h].astype(F32)).astype(BF16)
        if b != DIAG:
            m = MIRROR[b]
            send(lad.at[b, h], lad.at[4 + m, h], ls_sem.at[b, h], lr_sem.at[m, h], device(dz=DZ[b]))

    select_diagonal()
    for b in range(3):
        select_given(b)
    load_t.wait()
    picked = dot(tv[...], jnp.concatenate([sel[b] for b in range(3, 7)], axis=1)).astype(BF16)
    at[DIAG, y, here, :] = picked[:, :LANES]
    for b in range(3):
        zs[b] = picked[:, (1 + b) * LANES : (2 + b) * LANES]
    pl.semaphore_wait(barrier, len(partners))
    def give(b):
        send(zs.at[b], zr.at[MIRROR[b]], zs_sem.at[b], zr_sem.at[MIRROR[b]], device(dz=DZ[b]))

    give(0)
    give(1)
    to_neighbours(DIAG)
    to_next(DIAG, 0)
    to_previous(DIAG, 0)

    for b in range(3):
        select_kept(b)
    own[...] = dot(tv[...], jnp.concatenate([sel[b] for b in range(3)], axis=1))

    def antisymmetric(b):
        landed(zr.at[b], zr_sem.at[b])
        lanes = slice(b * LANES, (b + 1) * LANES)
        at[b, y, here, :] = (own[:, lanes] + zr[b].astype(F32)).astype(BF16)
        to_neighbours(b)

    turn(0)
    turn(1)
    share(DIAG, 3, 0)
    forward_diagonal(3, 0, device(dy=1))
    share(DIAG, 1, 0)
    forward_diagonal(1, 1, device(dy=3))
    from_x(DIAG)
    antisymmetric(0)
    to_next(0, 0)
    to_previous(0, 0)
    antisymmetric(1)
    to_next(1, 0)
    to_previous(1, 0)
    give(2)
    turn(2)
    turn(3)
    antisymmetric(2)
    across(1)
    across(3)
    share_diagonal()
    turn(4)
    from_x(0)
    to_previous(0, 2)
    to_next(0, 2)
    share(0, 3, 0)
    forward_next(0)
    share(0, 1, 0)
    multiply(DIAG, 0)
    multiply(0, 0)
    from_x(1)
    to_previous(1, 2)
    to_next(1, 2)
    share(1, 3, 0)
    forward_next(1)
    share(1, 1, 0)
    multiply(1, 0)
    from_x(2)
    to_next(2, 0)
    share(0, 1, 2)
    forward_previous(0)
    share(0, 3, 2)
    multiply(2, 0)
    multiply(0, 1)
    share(1, 1, 2)
    forward_previous(1)
    to_previous(2, 2)
    to_previous(2, 0)
    to_next(2, 2)
    share(0, 2, 0)
    from_x(DIAG, 1)
    multiply(0, 3)
    multiply(DIAG, 1)
    share(1, 3, 2)
    share(0, 2, 2)
    from_x(DIAG, 3)
    multiply(1, 1)
    multiply(0, 2)
    from_x(DIAG, 2)
    share(1, 2, 0)
    share(1, 2, 2)
    multiply(1, 3)
    multiply(DIAG, 3)
    share(2, 3, 0)
    forward_next(2)
    share(2, 1, 2)
    forward_previous(2)
    multiply(1, 2)
    multiply(DIAG, 2)
    share(2, 3, 2)
    share(2, 1, 0)
    multiply(2, 1)
    multiply(2, 3)
    share(2, 2, 0)
    share(2, 2, 2)
    finish(0, 0)
    finish(0, 1)
    multiply(2, 2)
    reduce(DIAG, 0)
    reduce(DIAG, 1)
    finish(1, 0)
    finish(1, 1)
    finish(2, 0)
    finish(2, 1)
    for h in range(2):
        finish(DIAG, h)
        for b in range(3):
            landed(lad.at[4 + b, h], lr_sem.at[b, h])
        parts = jnp.concatenate([lad[b, h] for b in range(7)], axis=1)
        for n in range(0, OCC, 256):
            places = jnp.concatenate([sel[b, n : n + 256, :] for b in range(7)], axis=1)
            out[h * PART : (h + 1) * PART, n : n + 256] = dot(parts, places, ((1,), (1,))).astype(BF16)

    for copy in sends:
        copy.wait_send()


def on_device(amplitudes, integrals):
    dma = pltpu.SemaphoreType.DMA
    ladder = pl.pallas_call(
        kernel,
        out_shape=jax.ShapeDtypeStruct((HALF, OCC), BF16),
        in_specs=[pl.BlockSpec(memory_space=pltpu.HBM)] * 2,
        out_specs=pl.BlockSpec(memory_space=pltpu.VMEM),
        scratch_shapes=[
            pltpu.VMEM((CHUNK, OCC), BF16),
            pltpu.VMEM((4 * GROUP, 2 * HALF), BF16),
            pltpu.VMEM((2, 2 * HALF, SLAB), BF16),
            pltpu.VMEM((7, OCC, LANES), BF16),
            pltpu.VMEM((CHUNK, 3 * LANES), F32),
            pltpu.VMEM((3, CHUNK, LANES), BF16),
            pltpu.VMEM((3, CHUNK, LANES), BF16),
            pltpu.VMEM((4, 4, GROUP, LANES), BF16),
            pltpu.VMEM((4, LANES, 2 * HALF), F32),
            pltpu.VMEM((4, 2 * HALF, LANES), F32),
            pltpu.VMEM((4, 2, PART, LANES), BF16),
            pltpu.VMEM((4, 2, PART, LANES), BF16),
            pltpu.VMEM((7, 2, PART, LANES), BF16),
            dma((3,)), dma((3,)), dma((3,)), dma((4, 15)), dma((4, 4, 4)), dma((2,)), dma((2,)),
            dma((4, 2)), dma((4, 2)), dma((3, 2)), dma((3, 2)),
        ],
        compiler_params=pltpu.CompilerParams(
            collective_id=0, has_side_effects=True, vmem_limit_bytes=60 * 2**20
        ),
        name="ladder",
    )(amplitudes.T, integrals.T)
    return ladder.T


def solution(mesh):
    placed = (P("occ", ("red", "int")), P("red", "int"))
    return jax.shard_map(
        on_device, mesh=mesh, in_specs=placed, out_specs=P("occ", ("int", "red")), check_vma=False
    )
```

time: 215 us -> 58.4 us (0.27)
  waiting for transfers between devices: 129 us -> 0 us
  Pallas kernels: 0 us -> 55.3 us
  matrix products: 29 us -> 0 us
  blocking collectives: 27.7 us -> 0 us
  between operations: 13.4 us -> 0.01 us
  local copies, waits for them, and re-layouts: 11.3 us -> 2.72 us
  other arithmetic: 3.58 us -> 0 us
    all_gather x1 -> x0, waiting for transfers between devices: 78.6 us -> none  [on_device(): lax.all_gather(amplitudes, 'int', axis=1, tiled=True)]
    pallas_call x0 -> x1, Pallas kernels: none -> 55.3 us  [on_device(): pl.pallas_call(kernel, out_shape=jax.ShapeDtypeStruct((HALF, OCC), BF16),...]
    reduce_scatter x1 -> x0, waiting for transfers between devices: 49.9 us -> none  [on_device(): lax.psum_scatter(partial_sum.astype(jnp.bfloat16), 'red', scatter_dimensi...]
    dot_general x1 -> x0, matrix products: 29 us -> none  [on_device(): jnp.dot(lax.all_gather(amplitudes, 'int', axis=1, tiled=True), integrals,...]
    all_to_all x1 -> x0, blocking collectives: 27.7 us -> none  [swapped(): lax.all_to_all(cube.astype(jnp.bfloat16), 'occ', split_axis=1, concat_axi...]
    reshape x3 -> x0, local copies, waits for them, and re-layouts: 6.88 us -> none  [mirror_rows(): return cube.reshape(rows, width)]
    convert_element_type x1 -> x0, other arithmetic: 3.19 us -> none  [final_pairs(): (summed - mirror_rows(summed, occ_count, swapped)).astype(jnp.bfloat16)]
    reduce_scatter x1 -> x0, local copies, waits for them, and re-layouts: 3.01 us -> none  [on_device(): lax.psum_scatter(partial_sum.astype(jnp.bfloat16), 'red', scatter_dimensi...]
  transfers between devices with their start and end apart: 2 -> 0, of which waited for: 2 -> 0; matrix products, arithmetic and copies ran while one was open for 0% -> 0% of each run, Pallas kernels for 0% -> 0%
where the time goes in v2:
time: 58.4 us; the launch traced here: 58 us
  Pallas kernels  55.3 us (95%)
  local copies, waits for them, and re-layouts  2.72 us (5%)
    pallas_call x1, Pallas kernels, on_device(): pl.pallas_call(kernel, out_shape=jax.ShapeDtypeStruct((HALF, OCC), BF16),...  55.3 us
    unnamed x1, local copies, waits for them, and re-layouts  2.72 us

profile of v2, /device:TPU:0, one launch (start us, length us, event | category | flops | bytes accessed | tf_op | source)
XLA Modules:
  0.0 58.0 jit_solution(18433052643517016868)
XLA Ops:
  0.0 55.3 %ladder.1 = bf16[800,1024]{1,0:T(8,128)(2,1)} custom-call(bf16[400,1024]{1,0:T(8,128)(2,1)} %bitcast.5, bf16[1600,6400]{1,0:T(8,128)(2,1)} %bitcast.3), custom_call_target="tpu_custom_call" | custom-call | tf_op jit(solution)/shard_map/ladder/pallas_call | solution.py:310
  55.3 2.7 %copy.4 = bf16[1024,800]{0,1:T(8,128)(2,1)} copy(bf16[1024,800]{0,1:T(8,128)(2,1)} %bitcast.4) | data formatting | bytes 3276800

commit v3 on v2

--- a/solution.py
+++ b/solution.py
@@ -15,7 +15,8 @@
 GROUP = 1600
 SLAB = 1280
 HALF = 800
-PART = 400
+HALVES = ((0, 400), (400, 400))
+PIECES = (HALVES, HALVES, ((0, 208), (208, 192), (400, 208), (608, 192)), HALVES)
 OCC = 1024
 DZ = (1, 3, 2, 0)
 MIRROR = (1, 0, 2)
@@ -26,8 +27,39 @@
     return lax.dot_general(a, b, (dims, ((), ())), preferred_element_type=F32)
 
 
+def selections(z, given, kept, put):
+    pair = lax.broadcasted_iota(I32, (1, LANES), 1)
+    row = lax.broadcasted_iota(I32, (OCC, LANES), 0)
+
+    def pairs_of(owner_is_lower):
+        a = jnp.where(owner_is_lower, pair >> 4, pair >> 3)
+        b = jnp.where(owner_is_lower, pair & 15, 8 + (pair & 7))
+        return a, b
+
+    for b in range(3):
+        other = (z + DZ[b]) % 4
+        if kept:
+            p, q = pairs_of(z < other)
+            put(b, jnp.where(row == p * 64 + other * 16 + q, 1.0, 0.0).astype(BF16))
+        if given:
+            p, q = pairs_of(other < z)
+            put(4 + b, jnp.where(row == q * 64 + other * 16 + p, -1.0, 0.0).astype(BF16))
+    if given:
+        p = pair & 15
+        q = (p + 1 + (pair >> 4)) & 15
+        plus = jnp.where(pair < 120, p * 64 + z * 16 + q, -1)
+        minus = jnp.where(pair < 120, q * 64 + z * 16 + p, -1)
+        put(DIAG, (jnp.where(row == plus, 1.0, 0.0) - jnp.where(row == minus, 1.0, 0.0)).astype(BF16))
+
+
+def store_kernel(ladder, out, sem):
+    copy = pltpu.make_async_copy(ladder, out, sem)
+    copy.start()
+    copy.wait()
+
+
 def kernel(
-    t_hbm, v_hbm, out, tv, vv, slabs, sel, own, zs, zr, at, acc, total, rs, rr, lad,
+    t_hbm, v_hbm, out, tv, vv, slabs, sel, own, zs, zr, at, acc, total, rs, rr, lad, got,
     load_sem, zs_sem, zr_sem, as_sem, ar_sem, ds_sem, dr_sem, rs_sem, rr_sem, ls_sem, lr_sem,
 ):
     index, z, xh = lax.axis_index("int"), lax.axis_index("occ"), lax.axis_index("red")
@@ -51,31 +83,6 @@
     partners += [device(flip_x=1), device(flip_c=1), device(flip_red=1)]
     for partner in partners:
         pl.semaphore_signal(barrier, inc=1, device_id=partner, device_id_type=MESH)
-
-    pair = lax.broadcasted_iota(I32, (1, LANES), 1)
-    row = lax.broadcasted_iota(I32, (OCC, LANES), 0)
-
-    def pairs_of(owner_is_lower):
-        a = jnp.where(owner_is_lower, pair >> 4, pair >> 3)
-        b = jnp.where(owner_is_lower, pair & 15, 8 + (pair & 7))
-        return a, b
-
-    def select_kept(b):
-        other = (z + DZ[b]) % 4
-        p, q = pairs_of(z < other)
-        sel[b] = jnp.where(row == p * 64 + other * 16 + q, 1.0, 0.0).astype(BF16)
-
-    def select_given(b):
-        other = (z + DZ[b]) % 4
-        p, q = pairs_of(other < z)
-        sel[4 + b] = jnp.where(row == q * 64 + other * 16 + p, -1.0, 0.0).astype(BF16)
-
-    def select_diagonal():
-        p = pair & 15
-        q = (p + 1 + (pair >> 4)) & 15
-        plus = jnp.where(pair < 120, p * 64 + z * 16 + q, -1)
-        minus = jnp.where(pair < 120, q * 64 + z * 16 + p, -1)
-        sel[DIAG] = (jnp.where(row == plus, 1.0, 0.0) - jnp.where(row == minus, 1.0, 0.0)).astype(BF16)
 
     def turn(n):
         load_v[n].wait()
@@ -165,25 +172,50 @@
             acc[b] += product
         else:
             total[b] = (acc[b] + product).T
-            for h in range(2):
-                rs[b, h] = total[b, pl.ds(pl.multiple_of(theirs + h * PART, 16), PART), :].astype(BF16)
+            for h, (start, rows) in enumerate(PIECES[b]):
+                rs[b, start : start + rows, :] = total[b, pl.ds(pl.multiple_of(theirs + start, 16), rows), :].astype(BF16)
                 if b != DIAG:
                     reduce(b, h)
 
+    def piece(ref, b, h):
+        start, rows = PIECES[b][h]
+        return ref.at[b, pl.ds(start, rows), :]
+
     def reduce(b, h):
-        send(rs.at[b, h], rr.at[b, h], rs_sem.at[b, h], rr_sem.at[b, h], device(flip_red=1))
+        send(piece(rs, b, h), piece(rr, b, h), rs_sem.at[b, h], rr_sem.at[b, h], device(flip_red=1))
+
+    def expand(blocks, h, first):
+        start, rows = HALVES[h]
+        half = slice(start, start + rows)
+        for b in blocks:
+            if b != DIAG:
+                for k, (first_row, _) in enumerate(PIECES[b]):
+                    if start <= first_row < start + rows:
+                        landed(piece(got, b, k), lr_sem.at[b, k])
+        parts = [lad[b, half, :] for b in blocks] + [got[b, half, :] for b in blocks if b != DIAG]
+        places = list(blocks) + [4 + b for b in blocks if b != DIAG]
+        parts = jnp.concatenate(parts, axis=1)
+        for n in range(0, OCC, 256):
+            where = jnp.concatenate([sel[b, n : n + 256, :] for b in places], axis=1)
+            placed = dot(parts, where, ((1,), (1,)))
+            if not first:
+                placed += out[half, n : n + 256].astype(F32)
+            out[half, n : n + 256] = placed.astype(BF16)
 
     def finish(b, h):
-        landed(rr.at[b, h], rr_sem.at[b, h])
-        rows = pl.ds(pl.multiple_of(mine + h * PART, 16), PART)
-        lad[b, h] = (total[b, rows, :] + rr[b, h].astype(F32)).astype(BF16)
+        landed(piece(rr, b, h), rr_sem.at[b, h])
+        start, rows = PIECES[b][h]
+        here = slice(start, start + rows)
+        lad[b, here, :] = (total[b, pl.ds(pl.multiple_of(mine + start, 16), rows), :] + rr[b, here, :].astype(F32)).astype(BF16)
         if b != DIAG:
             m = MIRROR[b]
-            send(lad.at[b, h], lad.at[4 + m, h], ls_sem.at[b, h], lr_sem.at[m, h], device(dz=DZ[b]))
-
-    select_diagonal()
-    for b in range(3):
-        select_given(b)
+            there = got.at[m, pl.ds(start, rows), :]
+            send(piece(lad, b, h), there, ls_sem.at[b, h], lr_sem.at[m, h], device(dz=DZ[b]))
+
+    def put(b, places):
+        sel[b] = places
+
+    selections(z, True, False, put)
     load_t.wait()
     picked = dot(tv[...], jnp.concatenate([sel[b] for b in range(3, 7)], axis=1)).astype(BF16)
     at[DIAG, y, here, :] = picked[:, :LANES]
@@ -199,8 +231,7 @@
     to_next(DIAG, 0)
     to_previous(DIAG, 0)
 
-    for b in range(3):
-        select_kept(b)
+    selections(z, False, True, put)
     own[...] = dot(tv[...], jnp.concatenate([sel[b] for b in range(3)], axis=1))
 
     def antisymmetric(b):
@@ -277,6 +308,7 @@
     forward_previous(2)
     multiply(1, 2)
     multiply(DIAG, 2)
+    reduce(DIAG, 0)
     share(2, 3, 2)
     share(2, 1, 0)
     multiply(2, 1)
@@ -286,20 +318,19 @@
     finish(0, 0)
     finish(0, 1)
     multiply(2, 2)
-    reduce(DIAG, 0)
     reduce(DIAG, 1)
     finish(1, 0)
     finish(1, 1)
     finish(2, 0)
     finish(2, 1)
-    for h in range(2):
-        finish(DIAG, h)
-        for b in range(3):
-            landed(lad.at[4 + b, h], lr_sem.at[b, h])
-        parts = jnp.concatenate([lad[b, h] for b in range(7)], axis=1)
-        for n in range(0, OCC, 256):
-            places = jnp.concatenate([sel[b, n : n + 256, :] for b in range(7)], axis=1)
-            out[h * PART : (h + 1) * PART, n : n + 256] = dot(parts, places, ((1,), (1,))).astype(BF16)
+    expand((0, 1), 0, True)
+    expand((0, 1), 1, True)
+    finish(2, 2)
+    finish(2, 3)
+    finish(DIAG, 0)
+    expand((2, DIAG), 0, False)
+    finish(DIAG, 1)
+    expand((2, DIAG), 1, False)
 
     for copy in sends:
         copy.wait_send()
@@ -309,7 +340,7 @@
     dma = pltpu.SemaphoreType.DMA
     ladder = pl.pallas_call(
         kernel,
-        out_shape=jax.ShapeDtypeStruct((HALF, OCC), BF16),
+        out_shape=pltpu.VMEM((HALF, OCC), BF16),
         in_specs=[pl.BlockSpec(memory_space=pltpu.HBM)] * 2,
         out_specs=pl.BlockSpec(memory_space=pltpu.VMEM),
         scratch_shapes=[
@@ -323,17 +354,26 @@
             pltpu.VMEM((4, 4, GROUP, LANES), BF16),
             pltpu.VMEM((4, LANES, 2 * HALF), F32),
             pltpu.VMEM((4, 2 * HALF, LANES), F32),
-            pltpu.VMEM((4, 2, PART, LANES), BF16),
-            pltpu.VMEM((4, 2, PART, LANES), BF16),
-            pltpu.VMEM((7, 2, PART, LANES), BF16),
+            pltpu.VMEM((4, HALF, LANES), BF16),
+            pltpu.VMEM((4, HALF, LANES), BF16),
+            pltpu.VMEM((4, HALF, LANES), BF16),
+            pltpu.VMEM((3, HALF, LANES), BF16),
             dma((3,)), dma((3,)), dma((3,)), dma((4, 15)), dma((4, 4, 4)), dma((2,)), dma((2,)),
-            dma((4, 2)), dma((4, 2)), dma((3, 2)), dma((3, 2)),
+            dma((4, 4)), dma((4, 4)), dma((3, 4)), dma((3, 4)),
         ],
         compiler_params=pltpu.CompilerParams(
-            collective_id=0, has_side_effects=True, vmem_limit_bytes=60 * 2**20
+            collective_id=0, has_side_effects=True, vmem_limit_bytes=117 * 2**19
         ),
         name="ladder",
     )(amplitudes.T, integrals.T)
+    ladder = pl.pallas_call(
+        store_kernel,
+        out_shape=jax.ShapeDtypeStruct((HALF, OCC), BF16),
+        in_specs=[pl.BlockSpec(memory_space=pltpu.VMEM)],
+        out_specs=pl.BlockSpec(memory_space=pltpu.HBM),
+        scratch_shapes=[pltpu.SemaphoreType.DMA],
+        name="store",
+    )(pltpu.with_memory_space_constraint(ladder, pltpu.VMEM))
     return ladder.T
 
 

time: 58.4 us -> 55.6 us (0.952)
  local copies, waits for them, and re-layouts: 2.72 us -> 0 us
    unnamed x1 -> x0, local copies, waits for them, and re-layouts: 2.72 us -> none
    pallas_call x1 -> x2, Pallas kernels: 55.3 us -> 55.2 us  [the longest x1 54.1 us: on_device(): pl.pallas_call(kernel, out_shape=pltpu.VMEM((HALF, OCC), BF16), in_specs=...]
where the time goes in v3:
time: 55.6 us; the launch traced here: 55.4 us
  Pallas kernels  55.2 us (99%)
    pallas_call x1, Pallas kernels, on_device(): pl.pallas_call(kernel, out_shape=pltpu.VMEM((HALF, OCC), BF16), in_specs=...  54.1 us
    pallas_call x1, Pallas kernels, on_device(): pl.pallas_call(store_kernel, out_shape=jax.ShapeDtypeStruct((HALF, OCC),...  1.17 us

profile of v3, /device:TPU:0, one launch (start us, length us, event | category | flops | bytes accessed | tf_op | source)
XLA Modules:
  0.0 55.4 jit_solution(831617843036646677)
XLA Ops:
  0.0 54.1 %ladder.1 = bf16[800,1024]{1,0:T(8,128)(2,1)S(1)} custom-call(bf16[400,1024]{1,0:T(8,128)(2,1)} %bitcast.4, bf16[1600,6400]{1,0:T(8,128)(2,1)} %bitcast.3), custom_call_target="tpu_custom_call" | custom-call | tf_op jit(solution)/shard_map/ladder/pallas_call | solution.py:341
  54.1 1.2 %store.1 = bf16[800,1024]{1,0:T(8,128)(2,1)} custom-call(bf16[800,1024]{1,0:T(8,128)(2,1)S(1)} %ladder.1), custom_call_target="tpu_custom_call" | custom-call | tf_op jit(solution)/shard_map/store/pallas_call | solution.py:369

commit v4 on v3

--- a/solution.py
+++ b/solution.py
@@ -1,5 +1,3 @@
-import functools
-
 import jax
 import jax.numpy as jnp
 from jax import lax
@@ -71,12 +69,12 @@
 
     load_t = pltpu.make_async_copy(t_hbm, tv, load_sem.at[0])
     load_v = [
-        pltpu.make_async_copy(v_hbm.at[:, n * SLAB : (n + 1) * SLAB], slabs.at[n % 2], load_sem.at[1 + n % 2])
+        pltpu.make_async_copy(v_hbm.at[:, n * SLAB : (n + 1) * SLAB], slabs.at[n % 4], load_sem.at[1 + n % 4])
         for n in range(4 * GROUP // SLAB)
     ]
     load_t.start()
-    load_v[0].start()
-    load_v[1].start()
+    for load in load_v[:4]:
+        load.start()
 
     barrier = pltpu.get_barrier_semaphore()
     partners = [device(dy=1), device(dy=3), device(dz=1), device(dz=2), device(dz=3)]
@@ -89,12 +87,12 @@
 
         def lanes(k, carry):
             first = pl.multiple_of(k * 128, 128)
-            vv[pl.ds(n * SLAB + first, 128), :] = slabs[n % 2, :, pl.ds(first, 128)].T
+            vv[pl.ds(n * SLAB + first, 128), :] = slabs[n % 4, :, pl.ds(first, 128)].T
             return carry
 
         lax.fori_loop(0, SLAB // 128, lanes, 0, unroll=2)
-        if n + 2 < len(load_v):
-            load_v[n + 2].start()
+        if n + 4 < len(load_v):
+            load_v[n + 4].start()
 
     sends = []
 
@@ -256,11 +254,11 @@
     give(2)
     turn(2)
     turn(3)
+    turn(4)
     antisymmetric(2)
     across(1)
     across(3)
     share_diagonal()
-    turn(4)
     from_x(0)
     to_previous(0, 2)
     to_next(0, 2)
@@ -281,7 +279,6 @@
     share(0, 1, 2)
     forward_previous(0)
     share(0, 3, 2)
-    multiply(2, 0)
     multiply(0, 1)
     share(1, 1, 2)
     forward_previous(1)
@@ -297,6 +294,7 @@
     from_x(DIAG, 3)
     multiply(1, 1)
     multiply(0, 2)
+    multiply(2, 0)
     from_x(DIAG, 2)
     share(1, 2, 0)
     share(1, 2, 2)
@@ -346,7 +344,7 @@
         scratch_shapes=[
             pltpu.VMEM((CHUNK, OCC), BF16),
             pltpu.VMEM((4 * GROUP, 2 * HALF), BF16),
-            pltpu.VMEM((2, 2 * HALF, SLAB), BF16),
+            pltpu.VMEM((4, 2 * HALF, SLAB), BF16),
             pltpu.VMEM((7, OCC, LANES), BF16),
             pltpu.VMEM((CHUNK, 3 * LANES), F32),
             pltpu.VMEM((3, CHUNK, LANES), BF16),
@@ -358,7 +356,7 @@
             pltpu.VMEM((4, HALF, LANES), BF16),
             pltpu.VMEM((4, HALF, LANES), BF16),
             pltpu.VMEM((3, HALF, LANES), BF16),
-            dma((3,)), dma((3,)), dma((3,)), dma((4, 15)), dma((4, 4, 4)), dma((2,)), dma((2,)),
+            dma((5,)), dma((3,)), dma((3,)), dma((4, 15)), dma((4, 4, 4)), dma((2,)), dma((2,)),
             dma((4, 4)), dma((4, 4)), dma((3, 4)), dma((3, 4)),
         ],
         compiler_params=pltpu.CompilerParams(

time: 55.6 us -> 55.4 us (level)
  no operation moved by 1% of the time
where the time goes in v4:
time: 55.4 us; the launch traced here: 55.3 us
  Pallas kernels  55.1 us (99%)
    pallas_call x1, Pallas kernels, on_device(): pl.pallas_call(kernel, out_shape=pltpu.VMEM((HALF, OCC), BF16), in_specs=...  54 us
    pallas_call x1, Pallas kernels, on_device(): pl.pallas_call(store_kernel, out_shape=jax.ShapeDtypeStruct((HALF, OCC),...  1.17 us

profile of v4, /device:TPU:0, one launch (start us, length us, event | category | flops | bytes accessed | tf_op | source)
XLA Modules:
  0.0 55.3 jit_solution(5765786928971340578)
XLA Ops:
  0.0 54.0 %ladder.1 = bf16[800,1024]{1,0:T(8,128)(2,1)S(1)} custom-call(bf16[400,1024]{1,0:T(8,128)(2,1)} %bitcast.4, bf16[1600,6400]{1,0:T(8,128)(2,1)} %bitcast.3), custom_call_target="tpu_custom_call" | custom-call | tf_op jit(solution)/shard_map/ladder/pallas_call | solution.py:339
  54.0 1.2 %store.1 = bf16[800,1024]{1,0:T(8,128)(2,1)} custom-call(bf16[800,1024]{1,0:T(8,128)(2,1)S(1)} %ladder.1), custom_call_target="tpu_custom_call" | custom-call | tf_op jit(solution)/shard_map/store/pallas_call | solution.py:367
